TPU v7x, 32 devices: a whole 2x2x4 slice. The times are simulated.
32 devices in a mesh: gx: 4 (over x, core), gy: 4 (over z), gz: 2 (over y).
Axes of the slice: x: 2, y: 2, z: 4, core: 2. Of those that a mesh axis runs over, the one named last changes fastest.
Arguments:
- field: float32 [64, 32, 512], P('gx', 'gz', 'gy'), may hold values from -6 to 6
Outputs:
- coefficients: float32 [64, 32, 512], P('gx', 'gz', 'gy')
All inputs are finite; a program needn't handle non-finite values.
Results may differ from a plain program's by a relative error of at most 0.00002.
Values sent between devices are 32-bit elements; how exact they have to be, the bound alone decides.
A program may use at most 64 MiB of HBM per device.

v0:
```python
import jax
import jax.numpy as jnp
from jax import lax
from jax.sharding import PartitionSpec as P

ALPHA = -1.586134342
BETA = -0.05298011854
GAMMA = 0.8829110762
DELTA = 0.4435068522
ZETA = 1.149604398


def padded_2(block, sides, width):
    for axis, dim in sides:
        count = lax.axis_size(axis)
        forward = [(i, i + 1) for i in range(count - 1)]
        backward = [(target, source) for source, target in forward]
        low = lax.ppermute(
            lax.slice_in_dim(block, block.shape[dim] - width, None, axis=dim), axis, forward
        )
        high = lax.ppermute(lax.slice_in_dim(block, 0, width, axis=dim), axis, backward)
        block = jnp.concatenate([low, block, high], axis=dim)
    return block


def piece(array, start, stop, dim):
    return lax.slice_in_dim(array, start, stop, axis=dim)


def lift_padded(padded, dim):
    total = padded.shape[dim]
    half = total // 2
    shape = padded.shape[:dim] + (half, 2) + padded.shape[dim + 1 :]
    pairs = padded.reshape(shape)
    even = lax.index_in_dim(pairs, 0, dim + 1, keepdims=False)
    odd = lax.index_in_dim(pairs, 1, dim + 1, keepdims=False)
    odd_one = piece(odd, 0, half - 1, dim) + ALPHA * (
        piece(even, 0, half - 1, dim) + piece(even, 1, half, dim)
    )
    even_two = piece(even, 1, half - 1, dim) + BETA * (
        piece(odd_one, 0, half - 2, dim) + piece(odd_one, 1, half - 1, dim)
    )
    odd_three = piece(odd_one, 1, half - 2, dim) + GAMMA * (
        piece(even_two, 0, half - 3, dim) + piece(even_two, 1, half - 2, dim)
    )
    even_four = piece(even_two, 1, half - 3, dim) + DELTA * (
        piece(odd_three, 0, half - 4, dim) + piece(odd_three, 1, half - 3, dim)
    )
    lowpass = even_four * ZETA
    highpass = piece(odd_three, 1, half - 3, dim) / ZETA
    joined = jnp.stack([lowpass, highpass], axis=dim + 1)
    out_shape = padded.shape[:dim] + (total - 8,) + padded.shape[dim + 1 :]
    return joined.reshape(out_shape)


def mirror(extended, dim, first, last, width):
    length = extended.shape[dim] - 2 * width
    left = jnp.where(
        first,
        lax.rev(piece(extended, width + 1, 2 * width + 1, dim), (dim,)),
        piece(extended, 0, width, dim),
    )
    right = jnp.where(
        last,
        lax.rev(piece(extended, length - 1, length + width - 1, dim), (dim,)),
        piece(extended, length + width, length + 2 * width, dim),
    )
    return jnp.concatenate([left, piece(extended, width, length + width, dim), right], axis=dim)


def at_ends(where, count):
    return (where == 0, where == count - 1)


def on_device(field):
    first_x, last_x = at_ends(lax.axis_index("gx"), lax.axis_size("gx"))
    first_y, last_y = at_ends(lax.axis_index("gy"), lax.axis_size("gy"))
    first_z, last_z = at_ends(lax.axis_index("gz"), lax.axis_size("gz"))
    extended = padded_2(field, (("gx", 0),), 4)
    level_one = lift_padded(mirror(extended, 0, first_x, last_x, 4), 0)
    extended = padded_2(level_one, (("gz", 1),), 4)
    level_one = lift_padded(mirror(extended, 1, first_z, last_z, 4), 1)
    extended = padded_2(level_one, (("gy", 2),), 4)
    level_one = lift_padded(mirror(extended, 2, first_y, last_y, 4), 2)
    coarse = level_one[::2, ::2, ::2]
    extended = padded_2(coarse, (("gx", 0),), 4)
    coarse = lift_padded(mirror(extended, 0, first_x, last_x, 4), 0)
    extended = padded_2(coarse, (("gz", 1),), 4)
    coarse = lift_padded(mirror(extended, 1, first_z, last_z, 4), 1)
    extended = padded_2(coarse, (("gy", 2),), 4)
    coarse = lift_padded(mirror(extended, 2, first_y, last_y, 4), 2)
    return level_one.at[::2, ::2, ::2].set(coarse)


def solution(mesh):
    placed = (P("gx", "gz", "gy"),)
    return jax.shard_map(
        on_device, mesh=mesh, in_specs=placed, out_specs=P("gx", "gz", "gy"), check_vma=False
    )
```

profile of v0, /device:TPU:1, one launch (start us, length us, event | category | flops | bytes accessed | tf_op | source)
XLA Modules:
  0.0 96.8 jit_solution(9777443351744092953)
XLA Ops:
  0.8 4.5 %collective-permute-start = (f32[4,16,128]{2,1,0:T(8,128)S(1)}, f32[4,16,128]{2,1,0:T(8,128)S(1)}, u32[]{:S(2)}, u32[]{:S(2)}) collective-permute-start(f32[4,16,128]{2,1,0:T(8,128)S(1)} %get-tuple-element.32), channel_id=1, source_target_pairs={{0,8},{8,16},{16,24},{1,9},{9,17},{17,25},{2,10},{10,18},{18,26},{... | collective-permute-start | bytes 98312 | tf_op jit(solution)/shard_map/ppermute | solution.py:18
  5.4 1.9 %collective-permute-start.1 = (f32[4,16,128]{2,1,0:T(8,128)S(1)}, f32[4,16,128]{2,1,0:T(8,128)S(1)}, u32[]{:S(2)}, u32[]{:S(2)}) collective-permute-start(f32[4,16,128]{2,1,0:T(8,128)S(1)} %get-tuple-element.33), channel_id=1, source_target_pairs={{8,0},{16,8},{24,16},{9,1},{17,9},{25,17},{10,2},{18,10},{26,18},{... | collective-permute-start | bytes 98312 | tf_op jit(solution)/shard_map/ppermute | solution.py:21
  7.3 3.3 %collective-permute-done.1 = f32[4,16,128]{2,1,0:T(8,128)S(1)} collective-permute-done((f32[4,16,128]{2,1,0:T(8,128)S(1)}, f32[4,16,128]{2,1,0:T(8,128)S(1)}, u32[]{:S(2)}, u32[]{:S(2)}) %collective-permute-start.1) | collective-permute-done | bytes 32800 | tf_op jit(solution)/shard_map/ppermute | solution.py:21
  12.4 3.1 %collective-permute-start.2 = (f32[16,4,128]{2,0,1:T(8,128)S(1)}, f32[16,4,128]{2,0,1:T(8,128)S(1)}, u32[]{:S(2)}, u32[]{:S(2)}) collective-permute-start(f32[16,4,128]{2,0,1:T(8,128)S(1)} %get-tuple-element.29), channel_id=1, source_target_pairs={{0,1},{2,3},{4,5},{6,7},{8,9},{10,11},{12,13},{14,15},{16,17},{18,... | collective-permute-start | bytes 98312 | tf_op jit(solution)/shard_map/ppermute | solution.py:18
  15.6 1.3 %collective-permute-start.3 = (f32[16,4,128]{2,0,1:T(8,128)S(1)}, f32[16,4,128]{2,0,1:T(8,128)S(1)}, u32[]{:S(2)}, u32[]{:S(2)}) collective-permute-start(f32[16,4,128]{2,0,1:T(8,128)S(1)} %get-tuple-element.27), channel_id=1, source_target_pairs={{1,0},{3,2},{5,4},{7,6},{9,8},{11,10},{13,12},{15,14},{17,16},{19,... | collective-permute-start | bytes 98312 | tf_op jit(solution)/shard_map/ppermute | solution.py:21
  16.9 3.3 %collective-permute-done.3 = f32[16,4,128]{2,0,1:T(8,128)S(1)} collective-permute-done((f32[16,4,128]{2,0,1:T(8,128)S(1)}, f32[16,4,128]{2,0,1:T(8,128)S(1)}, u32[]{:S(2)}, u32[]{:S(2)}) %collective-permute-start.3) | collective-permute-done | bytes 32800 | tf_op jit(solution)/shard_map/ppermute | solution.py:21
  20.6 3.2 %collective-permute-start.4 = (f32[16,16,4]{2,0,1:T(8,128)S(1)}, f32[16,16,4]{2,0,1:T(8,128)S(1)}, u32[]{:S(2)}, u32[]{:S(2)}) collective-permute-start(f32[16,16,4]{2,0,1:T(8,128)S(1)} %get-tuple-element.22), channel_id=1, source_target_pairs={{0,2},{2,4},{4,6},{1,3},{3,5},{5,7},{8,10},{10,12},{12,14},{9,11},... | collective-permute-start | bytes 12296 | tf_op jit(solution)/shard_map/ppermute | solution.py:18
  23.9 1.3 %collective-permute-start.5 = (f32[16,16,4]{2,0,1:T(8,128)S(1)}, f32[16,16,4]{2,0,1:T(8,128)S(1)}, u32[]{:S(2)}, u32[]{:S(2)}) collective-permute-start(f32[16,16,4]{2,0,1:T(8,128)S(1)} %get-tuple-element.23), channel_id=1, source_target_pairs={{2,0},{4,2},{6,4},{3,1},{5,3},{7,5},{10,8},{12,10},{14,12},{11,9},... | collective-permute-start | bytes 12296 | tf_op jit(solution)/shard_map/ppermute | solution.py:21
  25.3 1.5 %collective-permute-done.4 = f32[16,16,4]{2,0,1:T(8,128)S(1)} collective-permute-done((f32[16,16,4]{2,0,1:T(8,128)S(1)}, f32[16,16,4]{2,0,1:T(8,128)S(1)}, u32[]{:S(2)}, u32[]{:S(2)}) %collective-permute-start.4) | collective-permute-done | bytes 4128 | tf_op jit(solution)/shard_map/ppermute | solution.py:18
  26.9 4.4 %collective-permute-done.5 = f32[16,16,4]{2,0,1:T(8,128)S(1)} collective-permute-done((f32[16,16,4]{2,0,1:T(8,128)S(1)}, f32[16,16,4]{2,0,1:T(8,128)S(1)}, u32[]{:S(2)}, u32[]{:S(2)}) %collective-permute-start.5) | collective-permute-done | bytes 4128 | tf_op jit(solution)/shard_map/ppermute | solution.py:21
  32.8 5.3 %slice.409 = f32[8,8,64]{1,0,2:T(8,128)S(1)} slice(f32[16,16,128]{1,0,2:T(8,128)S(1)} %bitcast.59), slice={[0:16:2], [0:16:2], [0:128:2]} | slice | bytes 32768 | tf_op jit(solution)/shard_map/slice | solution.py:85
  38.2 3.1 %collective-permute-start.6 = (f32[4,8,64]{1,0,2:T(4,128)S(1)}, f32[4,8,64]{1,0,2:T(4,128)S(1)}, u32[]{:S(2)}, u32[]{:S(2)}) collective-permute-start(f32[4,8,64]{1,0,2:T(4,128)S(1)} %get-tuple-element.11), channel_id=1, source_target_pairs={{0,8},{8,16},{16,24},{1,9},{9,17},{17,25},{2,10},{10,18},{18,26},{... | collective-permute-start | bytes 24584 | tf_op jit(solution)/shard_map/ppermute | solution.py:18
  41.9 1.9 %collective-permute-start.7 = (f32[4,8,64]{1,0,2:T(4,128)S(1)}, f32[4,8,64]{1,0,2:T(4,128)S(1)}, u32[]{:S(2)}, u32[]{:S(2)}) collective-permute-start(f32[4,8,64]{1,0,2:T(4,128)S(1)} %get-tuple-element.12), channel_id=1, source_target_pairs={{8,0},{16,8},{24,16},{9,1},{17,9},{25,17},{10,2},{18,10},{26,18},{... | collective-permute-start | bytes 24584 | tf_op jit(solution)/shard_map/ppermute | solution.py:21
  44.1 4.1 %collective-permute-done.7 = f32[4,8,64]{1,0,2:T(4,128)S(1)} collective-permute-done((f32[4,8,64]{1,0,2:T(4,128)S(1)}, f32[4,8,64]{1,0,2:T(4,128)S(1)}, u32[]{:S(2)}, u32[]{:S(2)}) %collective-permute-start.7) | collective-permute-done | bytes 8224 | tf_op jit(solution)/shard_map/ppermute | solution.py:21
  48.4 1.3 %collective-permute-start.8 = (f32[8,4,64]{2,0,1:T(8,128)S(1)}, f32[8,4,64]{2,0,1:T(8,128)S(1)}, u32[]{:S(2)}, u32[]{:S(2)}) collective-permute-start(f32[8,4,64]{2,0,1:T(8,128)S(1)} %get-tuple-element.47), channel_id=1, source_target_pairs={{0,1},{2,3},{4,5},{6,7},{8,9},{10,11},{12,13},{14,15},{16,17},{18,... | collective-permute-start | bytes 24584 | tf_op jit(solution)/shard_map/ppermute | solution.py:18
  49.9 1.3 %collective-permute-start.9 = (f32[8,4,64]{2,0,1:T(8,128)S(1)}, f32[8,4,64]{2,0,1:T(8,128)S(1)}, u32[]{:S(2)}, u32[]{:S(2)}) collective-permute-start(f32[8,4,64]{2,0,1:T(8,128)S(1)} %get-tuple-element.45), channel_id=1, source_target_pairs={{1,0},{3,2},{5,4},{7,6},{9,8},{11,10},{13,12},{15,14},{17,16},{19,... | collective-permute-start | bytes 24584 | tf_op jit(solution)/shard_map/ppermute | solution.py:21
  51.2 3.2 %collective-permute-done.9 = f32[8,4,64]{2,0,1:T(8,128)S(1)} collective-permute-done((f32[8,4,64]{2,0,1:T(8,128)S(1)}, f32[8,4,64]{2,0,1:T(8,128)S(1)}, u32[]{:S(2)}, u32[]{:S(2)}) %collective-permute-start.9) | collective-permute-done | bytes 8224 | tf_op jit(solution)/shard_map/ppermute | solution.py:21
  54.5 3.2 %collective-permute-start.10 = (f32[8,8,4]{2,0,1:T(8,128)S(1)}, f32[8,8,4]{2,0,1:T(8,128)S(1)}, u32[]{:S(2)}, u32[]{:S(2)}) collective-permute-start(f32[8,8,4]{2,0,1:T(8,128)S(1)} %get-tuple-element.40), channel_id=1, source_target_pairs={{0,2},{2,4},{4,6},{1,3},{3,5},{5,7},{8,10},{10,12},{12,14},{9,11},... | collective-permute-start | bytes 3080 | tf_op jit(solution)/shard_map/ppermute | solution.py:18
  57.8 8.5 %copy.66 = f32[16,16,64,2]{3,2,1,0:T(8,128)} copy(f32[16,16,64,2]{1,0,2,3:T(8,128)S(1)} %pad_maximum_fusion) | data formatting | bytes 262144 | tf_op jit(solution)/shard_map/stack | solution.py:51
  66.3 6.9 %reshape.73 = f32[32768]{0:T(1024)S(1)} reshape(f32[16,16,64,2]{3,2,1,0:T(8,128)} %copy.66) | data formatting | bytes 262144
  73.3 1.3 %collective-permute-start.11 = (f32[8,8,4]{2,0,1:T(8,128)S(1)}, f32[8,8,4]{2,0,1:T(8,128)S(1)}, u32[]{:S(2)}, u32[]{:S(2)}) collective-permute-start(f32[8,8,4]{2,0,1:T(8,128)S(1)} %get-tuple-element.41), channel_id=1, source_target_pairs={{2,0},{4,2},{6,4},{3,1},{5,3},{7,5},{10,8},{12,10},{14,12},{11,9},... | collective-permute-start | bytes 3080 | tf_op jit(solution)/shard_map/ppermute | solution.py:21
  74.7 3.3 %collective-permute-done.11 = f32[8,8,4]{2,0,1:T(8,128)S(1)} collective-permute-done((f32[8,8,4]{2,0,1:T(8,128)S(1)}, f32[8,8,4]{2,0,1:T(8,128)S(1)}, u32[]{:S(2)}, u32[]{:S(2)}) %collective-permute-start.11) | collective-permute-done | bytes 1056 | tf_op jit(solution)/shard_map/ppermute | solution.py:21
  78.4 1.6 %copy.77 = f32[8,8,32,2]{3,2,1,0:T(8,128)S(1)} copy(f32[8,8,32,2]{1,0,2,3:T(8,128)S(1)} %pad_maximum_fusion.2) | data formatting | bytes 32768 | tf_op jit(solution)/shard_map/stack | solution.py:51
  80.5 15.6 %scatter_fusion = f32[32768]{0:T(1024)S(1)} fusion(f32[32768]{0:T(1024)S(1)} %reshape.73, s32[4096]{0:T(1024)S(1)} %reshape.95, f32[4096]{0:T(1024)S(1)} %reshape.97), kind=kCustom, calls=%fused_computation | custom fusion | bytes 65536
  (96 shorter events, 7.5 us)
Async XLA Ops:
  0.8 6.5 %collective-permute-start = (f32[4,16,128]{2,1,0:T(8,128)S(1)}, f32[4,16,128]{2,1,0:T(8,128)S(1)}, u32[]{:S(2)}, u32[]{:S(2)}) collective-permute-start(f32[4,16,128]{2,1,0:T(8,128)S(1)} %get-tuple-element.32), channel_id=1, source_target_pairs={{0,8},{8,16},{16,24},{1,9},{9,17},{17,25},{2,10},{10,18},{18,26},{... | collective-permute-start | bytes 98312 | tf_op jit(solution)/shard_map/ppermute | solution.py:18
  5.4 5.2 %collective-permute-start.1 = (f32[4,16,128]{2,1,0:T(8,128)S(1)}, f32[4,16,128]{2,1,0:T(8,128)S(1)}, u32[]{:S(2)}, u32[]{:S(2)}) collective-permute-start(f32[4,16,128]{2,1,0:T(8,128)S(1)} %get-tuple-element.33), channel_id=1, source_target_pairs={{8,0},{16,8},{24,16},{9,1},{17,9},{25,17},{10,2},{18,10},{26,18},{... | collective-permute-start | bytes 98312 | tf_op jit(solution)/shard_map/ppermute | solution.py:21
  12.4 4.5 %collective-permute-start.2 = (f32[16,4,128]{2,0,1:T(8,128)S(1)}, f32[16,4,128]{2,0,1:T(8,128)S(1)}, u32[]{:S(2)}, u32[]{:S(2)}) collective-permute-start(f32[16,4,128]{2,0,1:T(8,128)S(1)} %get-tuple-element.29), channel_id=1, source_target_pairs={{0,1},{2,3},{4,5},{6,7},{8,9},{10,11},{12,13},{14,15},{16,17},{18,... | collective-permute-start | bytes 98312 | tf_op jit(solution)/shard_map/ppermute | solution.py:18
  15.6 4.7 %collective-permute-start.3 = (f32[16,4,128]{2,0,1:T(8,128)S(1)}, f32[16,4,128]{2,0,1:T(8,128)S(1)}, u32[]{:S(2)}, u32[]{:S(2)}) collective-permute-start(f32[16,4,128]{2,0,1:T(8,128)S(1)} %get-tuple-element.27), channel_id=1, source_target_pairs={{1,0},{3,2},{5,4},{7,6},{9,8},{11,10},{13,12},{15,14},{17,16},{19,... | collective-permute-start | bytes 98312 | tf_op jit(solution)/shard_map/ppermute | solution.py:21
  20.6 6.3 %collective-permute-start.4 = (f32[16,16,4]{2,0,1:T(8,128)S(1)}, f32[16,16,4]{2,0,1:T(8,128)S(1)}, u32[]{:S(2)}, u32[]{:S(2)}) collective-permute-start(f32[16,16,4]{2,0,1:T(8,128)S(1)} %get-tuple-element.22), channel_id=1, source_target_pairs={{0,2},{2,4},{4,6},{1,3},{3,5},{5,7},{8,10},{10,12},{12,14},{9,11},... | collective-permute-start | bytes 12296 | tf_op jit(solution)/shard_map/ppermute | solution.py:18
  23.9 7.4 %collective-permute-start.5 = (f32[16,16,4]{2,0,1:T(8,128)S(1)}, f32[16,16,4]{2,0,1:T(8,128)S(1)}, u32[]{:S(2)}, u32[]{:S(2)}) collective-permute-start(f32[16,16,4]{2,0,1:T(8,128)S(1)} %get-tuple-element.23), channel_id=1, source_target_pairs={{2,0},{4,2},{6,4},{3,1},{5,3},{7,5},{10,8},{12,10},{14,12},{11,9},... | collective-permute-start | bytes 12296 | tf_op jit(solution)/shard_map/ppermute | solution.py:21
  32.7 8.7 %copy-start.2 = (s32[3]{0:T(128)S(1)}, s32[3]{0:T(128)}, u32[]{:S(2)}) copy-start(s32[3]{0:T(128)} %constant.26) | copy-start | bytes 40
  38.2 5.8 %collective-permute-start.6 = (f32[4,8,64]{1,0,2:T(4,128)S(1)}, f32[4,8,64]{1,0,2:T(4,128)S(1)}, u32[]{:S(2)}, u32[]{:S(2)}) collective-permute-start(f32[4,8,64]{1,0,2:T(4,128)S(1)} %get-tuple-element.11), channel_id=1, source_target_pairs={{0,8},{8,16},{16,24},{1,9},{9,17},{17,25},{2,10},{10,18},{18,26},{... | collective-permute-start | bytes 24584 | tf_op jit(solution)/shard_map/ppermute | solution.py:18
  41.9 7.9 %copy-start.1 = (s32[3]{0:T(128)S(1)}, s32[3]{0:T(128)}, u32[]{:S(2)}) copy-start(s32[3]{0:T(128)} %constant.11) | copy-start | bytes 40
  41.9 6.3 %collective-permute-start.7 = (f32[4,8,64]{1,0,2:T(4,128)S(1)}, f32[4,8,64]{1,0,2:T(4,128)S(1)}, u32[]{:S(2)}, u32[]{:S(2)}) collective-permute-start(f32[4,8,64]{1,0,2:T(4,128)S(1)} %get-tuple-element.12), channel_id=1, source_target_pairs={{8,0},{16,8},{24,16},{9,1},{17,9},{25,17},{10,2},{18,10},{26,18},{... | collective-permute-start | bytes 24584 | tf_op jit(solution)/shard_map/ppermute | solution.py:21
  48.4 2.7 %collective-permute-start.8 = (f32[8,4,64]{2,0,1:T(8,128)S(1)}, f32[8,4,64]{2,0,1:T(8,128)S(1)}, u32[]{:S(2)}, u32[]{:S(2)}) collective-permute-start(f32[8,4,64]{2,0,1:T(8,128)S(1)} %get-tuple-element.47), channel_id=1, source_target_pairs={{0,1},{2,3},{4,5},{6,7},{8,9},{10,11},{12,13},{14,15},{16,17},{18,... | collective-permute-start | bytes 24584 | tf_op jit(solution)/shard_map/ppermute | solution.py:18
  49.9 4.5 %collective-permute-start.9 = (f32[8,4,64]{2,0,1:T(8,128)S(1)}, f32[8,4,64]{2,0,1:T(8,128)S(1)}, u32[]{:S(2)}, u32[]{:S(2)}) collective-permute-start(f32[8,4,64]{2,0,1:T(8,128)S(1)} %get-tuple-element.45), channel_id=1, source_target_pairs={{1,0},{3,2},{5,4},{7,6},{9,8},{11,10},{13,12},{15,14},{17,16},{19,... | collective-permute-start | bytes 24584 | tf_op jit(solution)/shard_map/ppermute | solution.py:21
  54.5 20.1 %collective-permute-start.10 = (f32[8,8,4]{2,0,1:T(8,128)S(1)}, f32[8,8,4]{2,0,1:T(8,128)S(1)}, u32[]{:S(2)}, u32[]{:S(2)}) collective-permute-start(f32[8,8,4]{2,0,1:T(8,128)S(1)} %get-tuple-element.40), channel_id=1, source_target_pairs={{0,2},{2,4},{4,6},{1,3},{3,5},{5,7},{8,10},{10,12},{12,14},{9,11},... | collective-permute-start | bytes 3080 | tf_op jit(solution)/shard_map/ppermute | solution.py:18
  73.3 4.7 %collective-permute-start.11 = (f32[8,8,4]{2,0,1:T(8,128)S(1)}, f32[8,8,4]{2,0,1:T(8,128)S(1)}, u32[]{:S(2)}, u32[]{:S(2)}) collective-permute-start(f32[8,8,4]{2,0,1:T(8,128)S(1)} %get-tuple-element.41), channel_id=1, source_target_pairs={{2,0},{4,2},{6,4},{3,1},{5,3},{7,5},{10,8},{12,10},{14,12},{11,9},... | collective-permute-start | bytes 3080 | tf_op jit(solution)/shard_map/ppermute | solution.py:21
  96.1 0.7 copy-start
where the time goes:
time: 97.4 us; the launch traced here: 96.8 us
  local copies, waits for them, and re-layouts  42.5 us (44%)
  starting transfers between devices  27.5 us (28%)
  waiting for transfers between devices  23.1 us (24%)
  other arithmetic  2.96 us (3%)
    unnamed x9, local copies, waits for them, and re-layouts  23.2 us
    ppermute x6, waiting for transfers between devices, padded_2(): lax.ppermute(lax.slice_in_dim(block, 0, width, axis=dim), axis, backward)  21.5 us
    ppermute x6, starting transfers between devices, padded_2(): lax.ppermute(lax.slice_in_dim(block, block.shape[dim] - width, None, axis...  18.5 us
    another operation x6, local copies, waits for them, and re-layouts, lift_padded(): joined = jnp.stack([lowpass, highpass], axis=dim + 1)  10.3 us
    ppermute x6, starting transfers between devices, padded_2(): lax.ppermute(lax.slice_in_dim(block, 0, width, axis=dim), axis, backward)  9 us
    slice x2, local copies, waits for them, and re-layouts, on_device(): coarse = level_one[::2, ::2, ::2]  5.45 us
  transfers between devices with their start and end apart: 12, of which 7 were waited for; matrix products, arithmetic and copies ran while one was open for 17% of the time, Pallas kernels for 0%

commit v1 on v0

v1 whole, which is shorter than its diff:
```python
import functools

import jax
import jax.numpy as jnp
from jax import lax
from jax.experimental import pallas as pl
from jax.experimental.pallas import tpu as pltpu
from jax.sharding import PartitionSpec as P

ALPHA = -1.586134342
BETA = -0.05298011854
GAMMA = 0.8829110762
DELTA = 0.4435068522
ZETA = 1.149604398
MESH = pl.DeviceIdType.MESH

FAR_LOW, FAR_HIGH = 12, 9
NEAR_LOW, NEAR_HIGH = 4, 3


def replaced(array, at, source, condition):
    entry = jnp.where(condition, array[source : source + 1], array[at : at + 1])
    parts = [array[:at]] if at else []
    parts.append(entry)
    if at + 1 < array.shape[0]:
        parts.append(array[at + 1 :])
    return jnp.concatenate(parts, axis=0)


def neighbours(array):
    return array[:-1] + array[1:]


def lift(even, odd, low, half, first, last):
    at = low + half
    odd = odd + ALPHA * neighbours(replaced(even, at, at - 1, last))
    even = even[1:-1] + BETA * neighbours(replaced(odd, low - 1, low, first))
    at = at - 1
    odd = odd[1:-1] + GAMMA * neighbours(replaced(even, at, at - 1, last))
    even = even[1:-1] + DELTA * neighbours(replaced(odd, low - 2, low - 1, first))
    return even * ZETA, odd * (1.0 / ZETA)


def split(cells):
    count = cells.shape[0]
    pairs = cells[: count // 2 * 2].reshape((count // 2, 2) + cells.shape[1:])
    even, odd = pairs[:, 0], pairs[:, 1]
    if count % 2:
        even = jnp.concatenate([even, cells[count - 1 :]], axis=0)
    return even, odd


def joined(even, odd):
    count = even.shape[0]
    return jnp.stack([even, odd], axis=1).reshape((2 * count,) + even.shape[1:])


def one_level(cells, low, first, last, half):
    even, odd = split(cells)
    even, odd = lift(even, odd, low // 2, half, first, last)
    begin = low // 2 - 1
    return even, odd[begin : begin + half]


def lift_lanes(main, halo, stride, lane, first, last):
    width = main.shape[-1]
    phase = lane % (2 * stride)
    is_even, is_odd = phase == 0, phase == stride
    low_edge, high_edge = lane < stride, lane >= width - stride
    low_end = (lane == 0) & first
    high_end = (lane == width - stride) & last
    for coefficient, mask in (
        (ALPHA, is_odd), (BETA, is_even), (GAMMA, is_odd), (DELTA, is_even),
    ):
        weight = jnp.where(mask, coefficient, 0.0)
        main_low, halo_low = pltpu.roll(main, stride, 1), pltpu.roll(halo, stride, 1)
        main_high, halo_high = (
            pltpu.roll(main, width - stride, 1), pltpu.roll(halo, width - stride, 1),
        )
        left = jnp.where(low_edge, halo_low, main_low)
        right = jnp.where(high_edge, halo_high, main_high)
        around_halo = jnp.where(low_edge, main_low, halo_low) + jnp.where(
            high_edge, main_high, halo_high
        )
        around = jnp.where(low_end, right, left) + jnp.where(high_end, left, right)
        main = main + weight * around
        halo = halo + weight * around_halo
    scale = jnp.where(is_even, ZETA, 1.0 / ZETA)
    return main * scale, halo * scale


def packed(tiles, low, lane):
    width = tiles[0].shape[-1]
    room = 2 * low
    per = width // room
    packs = []
    for start in range(0, len(tiles), per):
        pack = None
        for place, tile in enumerate(tiles[start : start + per]):
            moved = pltpu.roll(tile, (place * room + low) % width, 1)
            pack = moved if pack is None else jnp.where(lane // room == place, moved, pack)
        packs.append(pack)
    return packs


def unpacked(packs, low, count):
    width = packs[0].shape[-1]
    room = 2 * low
    per = width // room
    return [
        pltpu.roll(packs[t // per], (2 * width - (t % per) * room - low) % width, 1)
        for t in range(count)
    ]


def kernel(sizes, field, out, wide, near, far, edges, from_low, from_high, load_sem, send_sem, recv_sem):
    nx, nz, ny = field.shape
    place = {axis: lax.axis_index(axis) for axis in sizes}
    first = {axis: place[axis] == 0 for axis in sizes}
    last = {axis: place[axis] == sizes[axis] - 1 for axis in sizes}

    load = pltpu.make_async_copy(field, wide.at[pl.ds(FAR_LOW, nx)], load_sem)
    load.start()

    barrier = pltpu.get_barrier_semaphore()
    arrivals = 0
    for axis in sizes:
        for end, step in ((first, -1), (last, 1)):
            arrivals = arrivals + jnp.where(end[axis], 0, 1)

            @pl.when(jnp.logical_not(end[axis]))
            def _():
                pl.semaphore_signal(
                    barrier, inc=1, device_id={axis: place[axis] + step}, device_id_type=MESH
                )

    pl.semaphore_wait(barrier, arrivals)

    def shift(slot, axis, step, source, target):
        copy = pltpu.make_async_remote_copy(
            src_ref=source,
            dst_ref=target,
            send_sem=send_sem.at[slot],
            recv_sem=recv_sem.at[slot],
            device_id={axis: place[axis] + step},
            device_id_type=MESH,
        )
        sends = jnp.logical_not(last[axis] if step > 0 else first[axis])
        receives = jnp.logical_not(first[axis] if step > 0 else last[axis])
        pl.when(sends)(copy.start)
        return (lambda: pl.when(receives)(copy.wait_recv)), (lambda: pl.when(sends)(copy.wait_send))

    sent = []

    def exchange(*moves):
        waits = []
        for move in moves:
            arrived, left = shift(*move)
            waits.append(arrived)
            sent.append(left)
        for wait in waits:
            wait()

    moves = (
        (0, "gx", 1, field.at[pl.ds(nx - FAR_LOW, FAR_LOW)], wide.at[pl.ds(0, FAR_LOW)]),
        (1, "gx", -1, field.at[pl.ds(0, FAR_HIGH)], wide.at[pl.ds(FAR_LOW + nx, FAR_HIGH)]),
    )
    exchange(*moves)
    load.wait()
    ends = first["gx"], last["gx"]
    coarse, high = one_level(wide[...], FAR_LOW, *ends, nx // 2)
    begin = FAR_LOW // 2 - 2
    low = coarse[begin : begin + nx // 2]
    coarse = joined(*one_level(coarse, NEAR_LOW, *ends, nx // 4))

    half = nx // 2
    near[NEAR_LOW : NEAR_LOW + nz, :half] = jnp.swapaxes(low, 0, 1)
    near[NEAR_LOW : NEAR_LOW + nz, half:] = jnp.swapaxes(high, 0, 1)
    far[FAR_LOW : FAR_LOW + nz] = jnp.swapaxes(coarse, 0, 1)
    exchange(
        (2, "gz", 1, near.at[pl.ds(nz, NEAR_LOW)], near.at[pl.ds(0, NEAR_LOW)]),
        (3, "gz", -1, near.at[pl.ds(NEAR_LOW, NEAR_HIGH)], near.at[pl.ds(NEAR_LOW + nz, NEAR_HIGH)]),
        (4, "gz", 1, far.at[pl.ds(nz, FAR_LOW)], far.at[pl.ds(0, FAR_LOW)]),
        (5, "gz", -1, far.at[pl.ds(FAR_LOW, FAR_HIGH)], far.at[pl.ds(FAR_LOW + nz, FAR_HIGH)]),
    )
    ends = first["gz"], last["gz"]
    fine = joined(*one_level(near[...], NEAR_LOW, *ends, nz // 2))
    coarse, _ = one_level(far[...], FAR_LOW, *ends, nz // 2)
    coarse = joined(*one_level(coarse, NEAR_LOW, *ends, nz // 4))

    lane = lax.broadcasted_iota(jnp.int32, (half, ny), 1)
    fine_tiles = [fine[z, p * half : (p + 1) * half] for z in range(nz) for p in range(2)]
    coarse_tiles = [coarse[z] for z in range(nz // 2)]
    fine_packs = packed(fine_tiles, NEAR_LOW, lane)
    coarse_packs = packed(coarse_tiles, 16, lane)
    split_at = len(fine_packs)
    for i, pack in enumerate(fine_packs + coarse_packs):
        edges[i] = pack
    exchange((6, "gy", 1, edges, from_low), (7, "gy", -1, edges, from_high))
    ends = first["gy"], last["gy"]
    beside = [
        jnp.where(lane % (2 * NEAR_LOW) < NEAR_LOW, from_low[i], from_high[i]) for i in range(split_at)
    ]
    halo = unpacked(beside, NEAR_LOW, len(fine_tiles))
    lane_at = lax.broadcasted_iota(jnp.int32, (1, ny), 1)
    fine, _ = lift_lanes(
        jnp.concatenate(fine_tiles, axis=0), jnp.concatenate(halo, axis=0), 1, lane_at, *ends
    )
    beside = [
        jnp.where(lane % 32 < 16, from_low[i], from_high[i])
        for i in range(split_at, split_at + len(coarse_packs))
    ]
    halo = unpacked(beside, 16, len(coarse_tiles))
    pair = lift_lanes(
        jnp.concatenate(coarse_tiles, axis=0), jnp.concatenate(halo, axis=0), 1, lane_at, *ends
    )
    coarse, _ = lift_lanes(*pair, 2, lane_at, *ends)

    fine = fine.reshape(nz // 2, 2, 2, half, ny)
    coarse = coarse.reshape(nz // 2, half, ny)
    merged = jnp.where(lane % 2 == 0, coarse, fine[:, 0, 0])
    low = joined(merged, fine[:, 1, 0])
    high = joined(fine[:, 0, 1], fine[:, 1, 1])
    out[...] = joined(jnp.swapaxes(low, 0, 1), jnp.swapaxes(high, 0, 1))
    for wait in sent:
        wait()


def on_device(sizes, field):
    nx, nz, ny = field.shape
    half = nx // 2
    count = nz * 2 * 2 * NEAR_LOW // ny + nz // 2 * 32 // ny
    return pl.pallas_call(
        functools.partial(kernel, sizes),
        out_shape=jax.ShapeDtypeStruct(field.shape, field.dtype),
        in_specs=[pl.BlockSpec(memory_space=pl.ANY)],
        out_specs=pl.BlockSpec(memory_space=pltpu.VMEM),
        scratch_shapes=[
            pltpu.VMEM((FAR_LOW + nx + FAR_HIGH, nz, ny), jnp.float32),
            pltpu.VMEM((NEAR_LOW + nz + NEAR_HIGH, nx, ny), jnp.float32),
            pltpu.VMEM((FAR_LOW + nz + FAR_HIGH, half, ny), jnp.float32),
            pltpu.VMEM((count, half, ny), jnp.float32),
            pltpu.VMEM((count, half, ny), jnp.float32),
            pltpu.VMEM((count, half, ny), jnp.float32),
            pltpu.SemaphoreType.DMA,
            pltpu.SemaphoreType.DMA((8,)),
            pltpu.SemaphoreType.DMA((8,)),
        ],
        compiler_params=pltpu.CompilerParams(
            collective_id=0, has_side_effects=True, vmem_limit_bytes=32 * 1024 * 1024
        ),
        cost_estimate=pl.CostEstimate(flops=4_000_000, bytes_accessed=1_000_000, transcendentals=0),
    )(field)


def solution(mesh):
    sizes = {axis: mesh.shape[axis] for axis in ("gx", "gz", "gy")}
    placed = P("gx", "gz", "gy")
    return jax.shard_map(
        functools.partial(on_device, sizes),
        mesh=mesh, in_specs=(placed,), out_specs=placed, check_vma=False,
    )
```

time: 97.4 us -> 15.7 us (0.16)
  local copies, waits for them, and re-layouts: 42.5 us -> 1.56 us
  starting transfers between devices: 27.5 us -> 0 us
  waiting for transfers between devices: 23.1 us -> 0 us
  Pallas kernels: 0 us -> 14 us
  other arithmetic: 2.96 us -> 0 us
    ppermute x12 -> x0, starting transfers between devices: 27.5 us -> none  [the longest x6 18.5 us: padded_2(): lax.ppermute(lax.slice_in_dim(block, block.shape[dim] - width, None, axis...]
    ppermute x12 -> x0, waiting for transfers between devices: 23.1 us -> none  [the longest x6 21.5 us: padded_2(): lax.ppermute(lax.slice_in_dim(block, 0, width, axis=dim), axis, backward)]
    unnamed x9 -> x3, local copies, waits for them, and re-layouts: 23.2 us -> 1.56 us
    pallas_call x0 -> x1, Pallas kernels: none -> 14 us  [on_device(): pl.pallas_call(functools.partial(kernel, sizes), out_shape=jax.ShapeDtype...]
    another operation x6 -> x0, local copies, waits for them, and re-layouts: 10.3 us -> none  [lift_padded(): joined = jnp.stack([lowpass, highpass], axis=dim + 1)]
    slice x10 -> x0, local copies, waits for them, and re-layouts: 6.68 us -> none  [the longest x2 5.45 us: on_device(): coarse = level_one[::2, ::2, ::2]]
    concatenate x6 -> x0, other arithmetic: 1.2 us -> none  [mirror(): jnp.concatenate([left, piece(extended, width, length + width, dim), right...]
  transfers between devices with their start and end apart: 12 -> 0, of which waited for: 7 -> 0; matrix products, arithmetic and copies ran while one was open for 17% -> 0% of each run, Pallas kernels for 0% -> 0%
where the time goes in v1:
time: 15.7 us; the launch traced here: 15.6 us
  Pallas kernels  14 us (89%)
  local copies, waits for them, and re-layouts  1.56 us (10%)
    pallas_call x1, Pallas kernels, on_device(): pl.pallas_call(functools.partial(kernel, sizes), out_shape=jax.ShapeDtype...  14 us
    unnamed x3, local copies, waits for them, and re-layouts  1.56 us

profile of v1, /device:TPU:1, one launch (start us, length us, event | category | flops | bytes accessed | tf_op | source)
XLA Modules:
  0.0 15.6 jit_solution(383757156009723988)
XLA Ops:
  0.0 0.0 copy-start
  0.0 0.9 %copy-done = f32[16,16,128]{2,1,0:T(8,128)S(1)} copy-done((f32[16,16,128]{2,1,0:T(8,128)S(1)}, f32[16,16,128]{2,1,0:T(8,128)}, u32[]{:S(2)}) %copy-start) | copy-done | bytes 131096
  0.9 14.0 %shard_map.17 = f32[16,16,128]{2,1,0:T(8,128)S(1)} custom-call(f32[16,16,128]{2,1,0:T(8,128)S(1)} %copy-done), custom_call_target="tpu_custom_call" | custom-call | flops 4000000 | bytes 1000000 | tf_op jit(solution)/shard_map/pallas_call | solution.py:233
  14.9 0.7 %copy.3 = f32[16,16,128]{2,1,0:T(8,128)} copy(f32[16,16,128]{2,1,0:T(8,128)S(1)} %shard_map.17) | data formatting | bytes 262144
Async XLA Ops:
  0.0 0.9 %copy-start = (f32[16,16,128]{2,1,0:T(8,128)S(1)}, f32[16,16,128]{2,1,0:T(8,128)}, u32[]{:S(2)}) copy-start(f32[16,16,128]{2,1,0:T(8,128)} %field.1) | copy-start | bytes 393220

commit v2 on v1

v2 whole, which is shorter than its diff:
```python
import functools

import jax
import jax.numpy as jnp
from jax import lax
from jax.experimental import pallas as pl
from jax.experimental.pallas import tpu as pltpu
from jax.sharding import PartitionSpec as P

ALPHA = -1.586134342
BETA = -0.05298011854
GAMMA = 0.8829110762
DELTA = 0.4435068522
ZETA = 1.149604398
MESH = pl.DeviceIdType.MESH

FAR_LOW, FAR_HIGH = 12, 9
NEAR_LOW, NEAR_HIGH = 4, 3
NEAR_ROOM, FAR_ROOM = 8, 32


def replaced(array, at, source, condition):
    entry = jnp.where(condition, array[source : source + 1], array[at : at + 1])
    parts = [array[:at]] if at else []
    parts.append(entry)
    if at + 1 < array.shape[0]:
        parts.append(array[at + 1 :])
    return jnp.concatenate(parts, axis=0)


def neighbours(array):
    return array[:-1] + array[1:]


def lift(even, odd, low, half, first, last):
    at = low + half
    odd = odd + ALPHA * neighbours(replaced(even, at, at - 1, last))
    even = even[1:-1] + BETA * neighbours(replaced(odd, low - 1, low, first))
    at = at - 1
    odd = odd[1:-1] + GAMMA * neighbours(replaced(even, at, at - 1, last))
    even = even[1:-1] + DELTA * neighbours(replaced(odd, low - 2, low - 1, first))
    return even * ZETA, odd * (1.0 / ZETA)


def split(cells):
    count = cells.shape[0]
    pairs = cells[: count // 2 * 2].reshape((count // 2, 2) + cells.shape[1:])
    even, odd = pairs[:, 0], pairs[:, 1]
    if count % 2:
        even = jnp.concatenate([even, cells[count - 1 :]], axis=0)
    return even, odd


def joined(even, odd):
    count = even.shape[0]
    return jnp.stack([even, odd], axis=1).reshape((2 * count,) + even.shape[1:])


def one_level(even, odd, low, first, last, half):
    even, odd = lift(even, odd, low // 2, half, first, last)
    begin = low // 2 - 1
    return even, odd[begin : begin + half]


def lift_lanes(main, halo, stride, lane, first, last):
    width = main.shape[-1]
    phase = lane % (2 * stride)
    is_even, is_odd = phase == 0, phase == stride
    low_edge, high_edge = lane < stride, lane >= width - stride
    low_end = (lane == 0) & first
    high_end = (lane == width - stride) & last
    for coefficient, mask in (
        (ALPHA, is_odd), (BETA, is_even), (GAMMA, is_odd), (DELTA, is_even),
    ):
        weight = jnp.where(mask, coefficient, 0.0)
        main_low, halo_low = pltpu.roll(main, stride, 1), pltpu.roll(halo, stride, 1)
        main_high, halo_high = (
            pltpu.roll(main, width - stride, 1), pltpu.roll(halo, width - stride, 1),
        )
        left = jnp.where(low_edge, halo_low, main_low)
        right = jnp.where(high_edge, halo_high, main_high)
        around_halo = jnp.where(low_edge, main_low, halo_low) + jnp.where(
            high_edge, main_high, halo_high
        )
        around = jnp.where(low_end, right, left) + jnp.where(high_end, left, right)
        main = main + weight * around
        halo = halo + weight * around_halo
    scale = jnp.where(is_even, ZETA, 1.0 / ZETA)
    return main * scale, halo * scale


def edge_pack(near, far, lane):
    width = lane.shape[-1]
    half = width // 2
    pack = None
    for slot in range(2):
        start = slot * half
        part = pltpu.roll(far[slot], start + NEAR_ROOM * 2 + FAR_ROOM // 2, 1)
        for p in range(2):
            at = start + NEAR_ROOM * p
            moved = pltpu.roll(near[slot][p], at + NEAR_ROOM // 2, 1)
            part = jnp.where((lane >= at) & (lane < at + NEAR_ROOM), moved, part)
        pack = part if pack is None else jnp.where(lane >= half, part, pack)
    return pack


def from_low_side(lane):
    at = lane % (lane.shape[-1] // 2)
    beside_near = (at < 2 * NEAR_ROOM) & (at % NEAR_ROOM < NEAR_ROOM // 2)
    return beside_near | ((at >= 2 * NEAR_ROOM) & (at < 2 * NEAR_ROOM + FAR_ROOM // 2))


def kernel(sizes, field, out, wide, near, far, edges, from_low, from_high, load_sem, send_sem, recv_sem):
    nx, nz, ny = field.shape
    place = {axis: lax.axis_index(axis) for axis in sizes}
    first = {axis: place[axis] == 0 for axis in sizes}
    last = {axis: place[axis] == sizes[axis] - 1 for axis in sizes}

    ways = [{axis: step} for axis in sizes for step in (-1, 1)]
    ways += [{"gz": up, "gy": step} for up in (-1, 1) for step in (-1, 1)]

    def exists(way):
        there = None
        for axis, step in way.items():
            inside = jnp.logical_not(last[axis] if step > 0 else first[axis])
            there = inside if there is None else there & inside
        return there

    def device(way):
        return {axis: place[axis] + step for axis, step in way.items()}

    barrier = pltpu.get_barrier_semaphore()
    arrivals = 0
    for way in ways:
        there = exists(way)
        arrivals = arrivals + jnp.where(there, 1, 0)

        @pl.when(there)
        def _():
            pl.semaphore_signal(barrier, inc=1, device_id=device(way), device_id_type=MESH)

    load = pltpu.make_async_copy(field, wide.at[pl.ds(FAR_LOW, nx)], load_sem)
    load.start()
    pl.semaphore_wait(barrier, arrivals)

    def shift(slot, way, source, target):
        copy = pltpu.make_async_remote_copy(
            src_ref=source,
            dst_ref=target,
            send_sem=send_sem.at[slot],
            recv_sem=recv_sem.at[slot],
            device_id=device(way),
            device_id_type=MESH,
        )
        sends = exists(way)
        receives = exists({axis: -step for axis, step in way.items()})
        pl.when(sends)(copy.start)
        return (lambda: pl.when(receives)(copy.wait_recv)), (lambda: pl.when(sends)(copy.wait_send))

    sent = []

    def exchange(*moves):
        waits = {}
        for move in moves:
            arrived, left = shift(*move)
            waits[move[0]] = arrived
            sent.append(left)
        return lambda *slots: [waits[slot]() for slot in slots]

    arrived = exchange(
        (0, {"gx": 1}, field.at[pl.ds(nx - FAR_LOW, FAR_LOW)], wide.at[pl.ds(0, FAR_LOW)]),
        (1, {"gx": -1}, field.at[pl.ds(0, FAR_HIGH)], wide.at[pl.ds(FAR_LOW + nx, FAR_HIGH)]),
    )
    arrived(0, 1)
    load.wait()
    ends = first["gx"], last["gx"]
    coarse, high = one_level(*split(wide[...]), FAR_LOW, *ends, nx // 2)
    begin = FAR_LOW // 2 - 2
    low = coarse[begin : begin + nx // 2]
    coarse = joined(*one_level(*split(coarse), NEAR_LOW, *ends, nx // 4))

    half, pairs = nx // 2, nz // 2
    lane = lax.broadcasted_iota(jnp.int32, (half, ny), 1)
    low, high, coarse = (jnp.swapaxes(part, 0, 1) for part in (low, high, coarse))
    near[NEAR_LOW : NEAR_LOW + nz, :half] = low
    near[NEAR_LOW : NEAR_LOW + nz, half:] = high
    far[FAR_LOW : FAR_LOW + nz] = coarse
    for pair in range(pairs):
        layers = (2 * pair, 2 * pair + 1)
        edges[pair] = edge_pack([(low[z], high[z]) for z in layers], [coarse[z] for z in layers], lane)
    moves = [
        (2, {"gz": 1}, near.at[pl.ds(nz, NEAR_LOW)], near.at[pl.ds(0, NEAR_LOW)]),
        (3, {"gz": -1}, near.at[pl.ds(NEAR_LOW, NEAR_HIGH)], near.at[pl.ds(NEAR_LOW + nz, NEAR_HIGH)]),
        (4, {"gz": 1}, far.at[pl.ds(nz, FAR_LOW)], far.at[pl.ds(0, FAR_LOW)]),
        (5, {"gz": -1}, far.at[pl.ds(FAR_LOW, FAR_HIGH)], far.at[pl.ds(FAR_LOW + nz, FAR_HIGH)]),
    ]
    below, above = FAR_LOW // 2, (FAR_HIGH + 1) // 2
    for slot, step, target in ((6, 1, from_low), (9, -1, from_high)):
        moves += [
            (slot, {"gy": step}, edges, target.at[pl.ds(below, pairs)]),
            (slot + 1, {"gz": 1, "gy": step}, edges.at[pl.ds(pairs - below, below)], target.at[pl.ds(0, below)]),
            (slot + 2, {"gz": -1, "gy": step}, edges.at[pl.ds(0, above)], target.at[pl.ds(below + pairs, above)]),
        ]
    arrived = exchange(*moves)

    ends = first["gz"], last["gz"]
    arrived(2, 3)
    fine = joined(*one_level(*split(near[...]), NEAR_LOW, *ends, pairs))
    arrived(4, 5)
    coarse, _ = one_level(*split(far[...]), FAR_LOW, *ends, pairs)
    coarse = joined(*one_level(*split(coarse), NEAR_LOW, *ends, nz // 4))
    arrived(*range(6, 12))
    beside = jnp.where(from_low_side(lane), from_low[...], from_high[...])
    turned = pltpu.roll(beside[:-1].reshape(-1, ny), ny // 2, 1).reshape(-1, half, ny)
    around, around_high = one_level(beside, turned, FAR_LOW, *ends, pairs)
    begin = FAR_LOW // 2 - 2
    around_fine = joined(around[begin : begin + pairs], around_high)
    around_coarse = joined(*one_level(*split(around), NEAR_LOW, *ends, nz // 4))

    fine = fine.reshape(nz, 2, half, ny)
    around_fine = around_fine.reshape(-1, ny)
    halo = jnp.stack(
        [
            pltpu.roll(around_fine, ny - NEAR_ROOM * p - NEAR_ROOM // 2, 1).reshape(nz, half, ny)
            for p in range(2)
        ],
        axis=1,
    )
    ends = first["gy"], last["gy"]
    lane_at = lax.broadcasted_iota(jnp.int32, (1, ny), 1)
    fine, _ = lift_lanes(fine.reshape(-1, ny), halo.reshape(-1, ny), 1, lane_at, *ends)
    halo = pltpu.roll(around_coarse.reshape(-1, ny), ny - 2 * NEAR_ROOM - FAR_ROOM // 2, 1)
    coarse, halo = lift_lanes(coarse.reshape(-1, ny), halo, 1, lane_at, *ends)
    coarse, _ = lift_lanes(coarse, halo, 2, lane_at, *ends)

    fine = fine.reshape(nz // 2, 2, 2, half, ny)
    coarse = coarse.reshape(nz // 2, half, ny)
    merged = jnp.where(lane % 2 == 0, coarse, fine[:, 0, 0])
    low = joined(merged, fine[:, 1, 0])
    high = joined(fine[:, 0, 1], fine[:, 1, 1])
    out[...] = joined(jnp.swapaxes(low, 0, 1), jnp.swapaxes(high, 0, 1))
    for wait in sent:
        wait()


def on_device(sizes, field):
    nx, nz, ny = field.shape
    half = nx // 2
    pairs = nz // 2
    around = FAR_LOW // 2 + pairs + (FAR_HIGH + 1) // 2
    return pl.pallas_call(
        functools.partial(kernel, sizes),
        out_shape=jax.ShapeDtypeStruct(field.shape, field.dtype),
        in_specs=[pl.BlockSpec(memory_space=pltpu.HBM)],
        out_specs=pl.BlockSpec(memory_space=pltpu.VMEM),
        scratch_shapes=[
            pltpu.VMEM((FAR_LOW + nx + FAR_HIGH, nz, ny), jnp.float32),
            pltpu.VMEM((NEAR_LOW + nz + NEAR_HIGH, nx, ny), jnp.float32),
            pltpu.VMEM((FAR_LOW + nz + FAR_HIGH, half, ny), jnp.float32),
            pltpu.VMEM((pairs, half, ny), jnp.float32),
            pltpu.VMEM((around, half, ny), jnp.float32),
            pltpu.VMEM((around, half, ny), jnp.float32),
            pltpu.SemaphoreType.DMA,
            pltpu.SemaphoreType.DMA((12,)),
            pltpu.SemaphoreType.DMA((12,)),
        ],
        compiler_params=pltpu.CompilerParams(
            collective_id=0, has_side_effects=True, vmem_limit_bytes=32 * 1024 * 1024
        ),
        cost_estimate=pl.CostEstimate(flops=4_000_000, bytes_accessed=1_000_000, transcendentals=0),
    )(field)


def solution(mesh):
    sizes = {axis: mesh.shape[axis] for axis in ("gx", "gz", "gy")}
    placed = P("gx", "gz", "gy")
    return jax.shard_map(
        functools.partial(on_device, sizes),
        mesh=mesh, in_specs=(placed,), out_specs=placed, check_vma=False,
    )
```

time: 15.7 us -> 14.1 us (0.90)
  Pallas kernels: 14 us -> 12.4 us
    pallas_call x1, Pallas kernels: 14 us -> 12.4 us  [on_device(): pl.pallas_call(functools.partial(kernel, sizes), out_shape=jax.ShapeDtype...]
where the time goes in v2:
time: 14.1 us; the launch traced here: 13.9 us
  Pallas kernels  12.4 us (88%)
  local copies, waits for them, and re-layouts  1.56 us (11%)
    pallas_call x1, Pallas kernels, on_device(): pl.pallas_call(functools.partial(kernel, sizes), out_shape=jax.ShapeDtype...  12.4 us
    unnamed x3, local copies, waits for them, and re-layouts  1.56 us

profile of v2, /device:TPU:1, one launch (start us, length us, event | category | flops | bytes accessed | tf_op | source)
XLA Modules:
  0.0 13.9 jit_solution(767474011710046582)
XLA Ops:
  0.0 0.0 copy-start
  0.0 0.9 %copy-done = f32[16,16,128]{2,1,0:T(8,128)S(1)} copy-done((f32[16,16,128]{2,1,0:T(8,128)S(1)}, f32[16,16,128]{2,1,0:T(8,128)}, u32[]{:S(2)}) %copy-start) | copy-done | bytes 131096
  0.9 12.4 %shard_map.17 = f32[16,16,128]{2,1,0:T(8,128)S(1)} custom-call(f32[16,16,128]{2,1,0:T(8,128)S(1)} %copy-done), custom_call_target="tpu_custom_call" | custom-call | flops 4000000 | bytes 1000000 | tf_op jit(solution)/shard_map/pallas_call | solution.py:251
  13.3 0.7 %copy.3 = f32[16,16,128]{2,1,0:T(8,128)} copy(f32[16,16,128]{2,1,0:T(8,128)S(1)} %shard_map.17) | data formatting | bytes 262144
Async XLA Ops:
  0.0 0.9 %copy-start = (f32[16,16,128]{2,1,0:T(8,128)S(1)}, f32[16,16,128]{2,1,0:T(8,128)}, u32[]{:S(2)}) copy-start(f32[16,16,128]{2,1,0:T(8,128)} %field.1) | copy-start | bytes 393220

commit v3 on v2

--- a/solution.py
+++ b/solution.py
@@ -2,6 +2,7 @@
 
 import jax
 import jax.numpy as jnp
+import numpy as np
 from jax import lax
 from jax.experimental import pallas as pl
 from jax.experimental.pallas import tpu as pltpu
@@ -62,31 +63,58 @@
     return even, odd[begin : begin + half]
 
 
-def lift_lanes(main, halo, stride, lane, first, last):
-    width = main.shape[-1]
-    phase = lane % (2 * stride)
-    is_even, is_odd = phase == 0, phase == stride
-    low_edge, high_edge = lane < stride, lane >= width - stride
-    low_end = (lane == 0) & first
-    high_end = (lane == width - stride) & last
-    for coefficient, mask in (
-        (ALPHA, is_odd), (BETA, is_even), (GAMMA, is_odd), (DELTA, is_even),
-    ):
-        weight = jnp.where(mask, coefficient, 0.0)
-        main_low, halo_low = pltpu.roll(main, stride, 1), pltpu.roll(halo, stride, 1)
-        main_high, halo_high = (
-            pltpu.roll(main, width - stride, 1), pltpu.roll(halo, width - stride, 1),
-        )
-        left = jnp.where(low_edge, halo_low, main_low)
-        right = jnp.where(high_edge, halo_high, main_high)
-        around_halo = jnp.where(low_edge, main_low, halo_low) + jnp.where(
-            high_edge, main_high, halo_high
-        )
-        around = jnp.where(low_end, right, left) + jnp.where(high_end, left, right)
-        main = main + weight * around
-        halo = halo + weight * around_halo
-    scale = jnp.where(is_even, ZETA, 1.0 / ZETA)
-    return main * scale, halo * scale
+def lift_rows(cells):
+    even, odd = cells[0::2], cells[1::2]
+    count = min(len(even) - 1, len(odd))
+    even, odd = even[: count + 1], odd[:count]
+    odd = odd + ALPHA * neighbours(even)
+    even = even[1:-1] + BETA * neighbours(odd)
+    odd = odd[1:-1] + GAMMA * neighbours(even)
+    even = even[1:-1] + DELTA * neighbours(odd)
+    return even * ZETA, odd[1:] / ZETA
+
+
+def mirrored_rows(cells, low, count, first, last):
+    cells = cells.copy()
+    if first:
+        for k in range(1, low + 1):
+            cells[low - k] = cells[low + k]
+    if last:
+        for k in range(1, len(cells) - low - count + 1):
+            cells[low + count - 1 + k] = cells[low + count - 1 - k]
+    return cells
+
+
+def y_matrices(ny):
+    cases = []
+    for case in range(4):
+        first, last = case % 2 == 1, case >= 2
+        matrices = np.zeros((5, ny, ny))
+        low, high = FAR_LOW, FAR_LOW
+        inputs = np.eye(low + ny + high)
+        cells = mirrored_rows(inputs, low, ny, first, last)
+        even, odd = lift_rows(cells)
+        begin = low // 2 - 2
+        one = np.zeros((ny, len(inputs)))
+        one[0::2] = even[begin : begin + ny // 2]
+        one[1::2] = odd[begin : begin + ny // 2]
+        coarse = mirrored_rows(even, begin, ny // 2, first, last)
+        even, odd = lift_rows(coarse)
+        two = np.zeros((ny, len(inputs)))
+        two[0::4] = even[begin // 2 - 2 :][: ny // 4]
+        two[2::4] = odd[begin // 2 - 2 :][: ny // 4]
+        one, two = one.T, two.T
+        matrices[0], matrices[3] = one[low : low + ny], two[low : low + ny]
+        room = NEAR_ROOM // 2
+        for p in range(2):
+            at = NEAR_ROOM * p
+            matrices[1 + p, at : at + room] = one[low - room : low]
+            matrices[1 + p, at + room : at + 2 * room] = one[low + ny : low + ny + room]
+        at, room = 2 * NEAR_ROOM, FAR_ROOM // 2
+        matrices[4, at + room - low : at + room] = two[:low]
+        matrices[4, at + room : at + room + high] = two[low + ny :]
+        cases.append(matrices)
+    return np.stack(cases).astype(np.float32)
 
 
 def edge_pack(near, far, lane):
@@ -104,13 +132,15 @@
     return pack
 
 
-def from_low_side(lane):
+def packed_sides(lane):
     at = lane % (lane.shape[-1] // 2)
-    beside_near = (at < 2 * NEAR_ROOM) & (at % NEAR_ROOM < NEAR_ROOM // 2)
-    return beside_near | ((at >= 2 * NEAR_ROOM) & (at < 2 * NEAR_ROOM + FAR_ROOM // 2))
-
-
-def kernel(sizes, field, out, wide, near, far, edges, from_low, from_high, load_sem, send_sem, recv_sem):
+    is_near, is_far = at < 2 * NEAR_ROOM, (at >= 2 * NEAR_ROOM) & (at < 2 * NEAR_ROOM + FAR_ROOM)
+    near_low = at % NEAR_ROOM < NEAR_ROOM // 2
+    far_low = at < 2 * NEAR_ROOM + FAR_ROOM // 2
+    return (is_near & near_low) | (is_far & far_low), (is_near & ~near_low) | (is_far & ~far_low)
+
+
+def kernel(sizes, field, matrices, out, wide, near, far, edges, from_low, from_high, held, load_sem, send_sem, recv_sem):
     nx, nz, ny = field.shape
     place = {axis: lax.axis_index(axis) for axis in sizes}
     first = {axis: place[axis] == 0 for axis in sizes}
@@ -139,8 +169,12 @@
         def _():
             pl.semaphore_signal(barrier, inc=1, device_id=device(way), device_id_type=MESH)
 
-    load = pltpu.make_async_copy(field, wide.at[pl.ds(FAR_LOW, nx)], load_sem)
+    load = pltpu.make_async_copy(field, wide.at[pl.ds(FAR_LOW, nx)], load_sem.at[0])
     load.start()
+    case = jnp.where(first["gy"], 1, 0) + jnp.where(last["gy"], 2, 0)
+    fetch = pltpu.make_async_copy(matrices.at[case], held, load_sem.at[1])
+    fetch.start()
+    load.wait()
     pl.semaphore_wait(barrier, arrivals)
 
     def shift(slot, way, source, target):
@@ -168,11 +202,10 @@
         return lambda *slots: [waits[slot]() for slot in slots]
 
     arrived = exchange(
-        (0, {"gx": 1}, field.at[pl.ds(nx - FAR_LOW, FAR_LOW)], wide.at[pl.ds(0, FAR_LOW)]),
-        (1, {"gx": -1}, field.at[pl.ds(0, FAR_HIGH)], wide.at[pl.ds(FAR_LOW + nx, FAR_HIGH)]),
+        (0, {"gx": 1}, wide.at[pl.ds(nx, FAR_LOW)], wide.at[pl.ds(0, FAR_LOW)]),
+        (1, {"gx": -1}, wide.at[pl.ds(FAR_LOW, FAR_HIGH)], wide.at[pl.ds(FAR_LOW + nx, FAR_HIGH)]),
     )
     arrived(0, 1)
-    load.wait()
     ends = first["gx"], last["gx"]
     coarse, high = one_level(*split(wide[...]), FAR_LOW, *ends, nx // 2)
     begin = FAR_LOW // 2 - 2
@@ -210,34 +243,32 @@
     coarse, _ = one_level(*split(far[...]), FAR_LOW, *ends, pairs)
     coarse = joined(*one_level(*split(coarse), NEAR_LOW, *ends, nz // 4))
     arrived(*range(6, 12))
-    beside = jnp.where(from_low_side(lane), from_low[...], from_high[...])
+    low_side, high_side = packed_sides(lane)
+    low_side, high_side = low_side & ~first["gy"], high_side & ~last["gy"]
+    beside = jnp.where(low_side, from_low[...], jnp.where(high_side, from_high[...], 0.0))
     turned = pltpu.roll(beside[:-1].reshape(-1, ny), ny // 2, 1).reshape(-1, half, ny)
     around, around_high = one_level(beside, turned, FAR_LOW, *ends, pairs)
     begin = FAR_LOW // 2 - 2
     around_fine = joined(around[begin : begin + pairs], around_high)
     around_coarse = joined(*one_level(*split(around), NEAR_LOW, *ends, nz // 4))
 
-    fine = fine.reshape(nz, 2, half, ny)
-    around_fine = around_fine.reshape(-1, ny)
-    halo = jnp.stack(
-        [
-            pltpu.roll(around_fine, ny - NEAR_ROOM * p - NEAR_ROOM // 2, 1).reshape(nz, half, ny)
-            for p in range(2)
-        ],
-        axis=1,
-    )
-    ends = first["gy"], last["gy"]
-    lane_at = lax.broadcasted_iota(jnp.int32, (1, ny), 1)
-    fine, _ = lift_lanes(fine.reshape(-1, ny), halo.reshape(-1, ny), 1, lane_at, *ends)
-    halo = pltpu.roll(around_coarse.reshape(-1, ny), ny - 2 * NEAR_ROOM - FAR_ROOM // 2, 1)
-    coarse, halo = lift_lanes(coarse.reshape(-1, ny), halo, 1, lane_at, *ends)
-    coarse, _ = lift_lanes(coarse, halo, 2, lane_at, *ends)
-
-    fine = fine.reshape(nz // 2, 2, 2, half, ny)
-    coarse = coarse.reshape(nz // 2, half, ny)
-    merged = jnp.where(lane % 2 == 0, coarse, fine[:, 0, 0])
-    low = joined(merged, fine[:, 1, 0])
-    high = joined(fine[:, 0, 1], fine[:, 1, 1])
+    fetch.wait()
+
+    def times(cells, edge_cells, cell_matrix, edge_matrix):
+        cells = jnp.concatenate([cells.reshape(-1, ny), edge_cells.reshape(-1, ny)], axis=1)
+        matrix = jnp.concatenate([held[cell_matrix], held[edge_matrix]], axis=0)
+        return jnp.dot(
+            cells, matrix, precision=lax.Precision.HIGHEST, preferred_element_type=jnp.float32
+        ).reshape(-1, half, ny)
+
+    fine = [
+        times(fine[:, p * half : (p + 1) * half], around_fine, 0, 1 + p).reshape(pairs, 2, half, ny)
+        for p in range(2)
+    ]
+    coarse = times(coarse, around_coarse, 3, 4)
+
+    low = joined(jnp.where(lane % 2 == 0, coarse, fine[0][:, 0]), fine[0][:, 1])
+    high = fine[1].reshape(nz, half, ny)
     out[...] = joined(jnp.swapaxes(low, 0, 1), jnp.swapaxes(high, 0, 1))
     for wait in sent:
         wait()
@@ -251,7 +282,7 @@
     return pl.pallas_call(
         functools.partial(kernel, sizes),
         out_shape=jax.ShapeDtypeStruct(field.shape, field.dtype),
-        in_specs=[pl.BlockSpec(memory_space=pltpu.HBM)],
+        in_specs=[pl.BlockSpec(memory_space=pltpu.HBM)] * 2,
         out_specs=pl.BlockSpec(memory_space=pltpu.VMEM),
         scratch_shapes=[
             pltpu.VMEM((FAR_LOW + nx + FAR_HIGH, nz, ny), jnp.float32),
@@ -260,15 +291,16 @@
             pltpu.VMEM((pairs, half, ny), jnp.float32),
             pltpu.VMEM((around, half, ny), jnp.float32),
             pltpu.VMEM((around, half, ny), jnp.float32),
-            pltpu.SemaphoreType.DMA,
+            pltpu.VMEM((5, ny, ny), jnp.float32),
+            pltpu.SemaphoreType.DMA((2,)),
             pltpu.SemaphoreType.DMA((12,)),
             pltpu.SemaphoreType.DMA((12,)),
         ],
         compiler_params=pltpu.CompilerParams(
-            collective_id=0, has_side_effects=True, vmem_limit_bytes=32 * 1024 * 1024
+            collective_id=0, has_side_effects=True, vmem_limit_bytes=63488 * 1024
         ),
         cost_estimate=pl.CostEstimate(flops=4_000_000, bytes_accessed=1_000_000, transcendentals=0),
-    )(field)
+    )(field, jnp.asarray(y_matrices(ny)))
 
 
 def solution(mesh):

time: 14.1 us -> 13.7 us (0.972)
  Pallas kernels: 12.4 us -> 12 us
    pallas_call x1, Pallas kernels: 12.4 us -> 12 us  [on_device(): pl.pallas_call(functools.partial(kernel, sizes), out_shape=jax.ShapeDtype...]
    unnamed x3 -> x1, local copies, waits for them, and re-layouts: 1.56 us -> 1.57 us
where the time goes in v3:
time: 13.7 us; the launch traced here: 13.5 us
  Pallas kernels  12 us (88%)
  local copies, waits for them, and re-layouts  1.57 us (11%)
    pallas_call x1, Pallas kernels, on_device(): pl.pallas_call(functools.partial(kernel, sizes), out_shape=jax.ShapeDtype...  12 us
    unnamed x1, local copies, waits for them, and re-layouts  1.57 us

profile of v3, /device:TPU:1, one launch (start us, length us, event | category | flops | bytes accessed | tf_op | source)
XLA Modules:
  0.0 13.5 jit_solution(13773615569866038672)
XLA Ops:
  0.0 12.0 %shard_map.28 = f32[16,16,128]{2,1,0:T(8,128)} custom-call(f32[16,16,128]{2,1,0:T(8,128)} %field.1, f32[4,5,128,128]{3,2,1,0:T(8,128)} %constant.2.clone.matrices), custom_call_target="tpu_custom_call" | custom-call | flops 4000000 | bytes 1000000 | tf_op jit(solution)/shard_map/pallas_call | solution.py:282
  12.0 1.6 %copy.4 = f32[16,16,128]{2,1,0:T(8,128)} copy(f32[16,16,128]{2,1,0:T(8,128)} %shard_map.28) | data formatting | bytes 262144
